TPU v7x, 32 devices: a whole 2x2x4 slice. The times are simulated.
32 devices in a mesh: dp: 4 (over y, x), mp: 8 (over z, core).
Axes of the slice: x: 2, y: 2, z: 4, core: 2. Of those that a mesh axis runs over, the one named last changes fastest.
Arguments:
- emb_grad: bfloat16 [76032, 3584], P('mp', 'dp'), may hold values from -70 to 70
- emb_mom: bfloat16 [8, 4, 4, 2376, 896], P('mp', None, 'dp'), may hold values from -0.29882812 to 0.29882812
- blk_grad: bfloat16 [2, 3584, 18944], P(None, 'dp', 'mp'), may hold values from -70 to 70
- blk_mom: bfloat16 [2, 8, 3584, 2368], P(None, None, ('dp', 'mp')), may hold values from -0.29882812 to 0.29882812
- tile_group: int32 [2, 8, 8], replicated, may hold values from 1 to 3
- clip_rms: float32 [4], replicated, may hold values from 0.05 to 80
Outputs:
- emb_update: bfloat16 [8, 4, 4, 2376, 896], P('mp', None, 'dp')
- emb_moment: bfloat16 [8, 4, 4, 2376, 896], P('mp', None, 'dp')
- blk_update: bfloat16 [2, 8, 3584, 2368], P(None, None, ('dp', 'mp'))
- blk_moment: bfloat16 [2, 8, 3584, 2368], P(None, None, ('dp', 'mp'))
All inputs are finite; a program needn't handle non-finite values.
Results may differ from a plain program's by a relative error of at most 0.001.
Values may be sent and summed in bfloat16 or wider, within the bound.
A program may use at most 192 MiB of HBM per device.

v0:
```python
import jax
import jax.numpy as jnp
from jax import lax
from jax.sharding import PartitionSpec as P

beta_first = 0.9
beta_second = 0.99
temper = 0.05
epsilon = 1e-06


def lion_step(clipped, moment):
    moment = moment.astype(jnp.float32)
    update = jnp.tanh((beta_first * moment + (1.0 - beta_first) * clipped) / temper).astype(
        jnp.bfloat16
    )
    new_moment = (beta_second * moment + (1.0 - beta_second) * clipped).astype(jnp.bfloat16)
    return (update, new_moment)


def on_device(emb_grad, emb_mom, blk_grad, blk_mom, tile_group, clip_rms):
    dp_count = lax.axis_size("dp")
    mp_count = lax.axis_size("mp")
    dp_index = lax.axis_index("dp")
    mp_index = lax.axis_index("mp")
    groups = clip_rms.shape[0]
    tile_rows, tile_cols = emb_grad.shape
    own_rows = emb_mom.shape[3]
    feature_block = emb_mom.shape[4]
    matrices, block_rows, block_cols = blk_grad.shape
    owner_rows = blk_mom.shape[2]
    row_blocks = tile_group.shape[1] // dp_count
    block_height = block_rows // row_blocks
    labels = jnp.arange(groups, dtype=jnp.int32)
    first = (labels == 0).astype(jnp.float32)
    onehot = (tile_group[..., None] == labels).astype(jnp.float32)
    counts = jnp.sum(onehot, axis=(0, 1, 2)) * float(block_height * block_cols) + first * float(
        tile_rows * mp_count * tile_cols * dp_count
    )
    owner_block = dp_index * row_blocks + mp_index * owner_rows // block_height
    owner_ids = lax.dynamic_index_in_dim(onehot, owner_block, axis=1, keepdims=False)
    grad_pieces = blk_grad.reshape(matrices, mp_count, owner_rows, block_cols)
    blk_owner = lax.all_to_all(grad_pieces, "mp", split_axis=1, concat_axis=1, tiled=True)
    emb_pieces = emb_grad.reshape(dp_count, own_rows, feature_block)
    mom_local = emb_mom.reshape(dp_count, own_rows, feature_block)
    emb_owner = lax.all_to_all(emb_pieces, "dp", split_axis=0, concat_axis=0, tiled=True)
    emb_squares = jnp.sum(jnp.square(emb_grad.astype(jnp.float32)))
    block_squares = jnp.sum(
        jnp.square(blk_grad.astype(jnp.float32)).reshape(
            matrices, row_blocks, block_height, block_cols
        ),
        axis=(2, 3),
    )
    tile_rows_ids = lax.dynamic_slice_in_dim(onehot, dp_index * row_blocks, row_blocks, axis=1)
    tile_ids = lax.dynamic_index_in_dim(tile_rows_ids, mp_index, axis=2, keepdims=False)
    block_terms = jnp.sum(block_squares[..., None] * tile_ids, axis=(0, 1))
    partial_value = block_terms + emb_squares * first
    totals = lax.psum(partial_value, ("dp", "mp"))
    root_mean = jnp.sqrt(totals / jnp.maximum(counts, 1.0))
    factor = jnp.minimum(1.0, clip_rms / (root_mean + epsilon))
    owner_factor = jnp.sum(owner_ids * factor, axis=-1)
    clipped = blk_owner.astype(jnp.float32) * owner_factor[:, :, None, None]
    blk_update, blk_moment = lion_step(clipped, blk_mom)
    emb_update, emb_moment = lion_step(emb_owner.astype(jnp.float32) * factor[0], mom_local)
    return (
        emb_update.reshape(emb_mom.shape),
        emb_moment.reshape(emb_mom.shape),
        blk_update,
        blk_moment,
    )


def solution(mesh):
    placed = (
        P("mp", "dp"),
        P("mp", None, "dp", None, None),
        P(None, "dp", "mp"),
        P(None, None, ("dp", "mp"), None),
        P(),
        P(),
    )
    return jax.shard_map(
        on_device,
        mesh=mesh,
        in_specs=placed,
        out_specs=(
            P("mp", None, "dp", None, None),
            P("mp", None, "dp", None, None),
            P(None, None, ("dp", "mp"), None),
            P(None, None, ("dp", "mp"), None),
        ),
        check_vma=False,
    )
```

profile of v0, /device:TPU:9, one launch (start us, length us, event | category | flops | bytes accessed | tf_op | source)
XLA Modules:
  0.0 464.6 jit_solution(9423012465429596542)
XLA Ops:
  0.6 7.1 %all-to-all-start = ((bf16[4,2376,896]{2,1,0:T(8,128)(2,1)}), bf16[4,2376,896]{2,1,0:T(8,128)(2,1)}, u32[]{:S(2)}, u32[]{:S(2)}) async-start(bf16[4,2376,896]{2,1,0:T(8,128)(2,1)} %bitcast.39), calls=%async_computation | async-start | bytes 34062336 | tf_op jit(solution)/shard_map/all_to_all | solution.py:46
  7.7 12.5 %copy.41 = bf16[2,896,2368]{2,1,0:T(8,128)(2,1)} copy(bf16[2,896,2368]{1,2,0:T(8,128)(2,1)} %param.8) | data formatting | bytes 16973824 | tf_op args[2]
  20.2 0.0 copy-start
  20.2 7.6 %copy.42 = bf16[2,8,112,2368]{3,2,0,1:T(8,128)(2,1)} copy(bf16[2,8,112,2368]{3,2,1,0:T(8,128)(2,1)} %bitcast.40) | data formatting | bytes 16973824 | tf_op jit(solution)/shard_map/reshape | solution.py:42
  27.8 164.4 %all-to-all-done = bf16[4,2376,896]{2,1,0:T(8,128)(2,1)} async-done(((bf16[4,2376,896]{2,1,0:T(8,128)(2,1)}), bf16[4,2376,896]{2,1,0:T(8,128)(2,1)}, u32[]{:S(2)}, u32[]{:S(2)}) %all-to-all-start) | async-done | bytes 17031200 | tf_op jit(solution)/shard_map/all_to_all | solution.py:46
  192.1 6.4 %all-to-all-start.1 = ((bf16[2,8,112,2368]{3,2,0,1:T(8,128)(2,1)}), bf16[2,8,112,2368]{3,2,0,1:T(8,128)(2,1)}, u32[]{:S(2)}, u32[]{:S(2)}) async-start(bf16[2,8,112,2368]{3,2,0,1:T(8,128)(2,1)} %copy.42), calls=%async_computation.1 | async-start | bytes 17432576 | tf_op jit(solution)/shard_map/all_to_all | solution.py:43
  198.6 0.0 copy-start.1
  198.6 0.0 copy-done
  198.6 0.1 constant_dynamic-slice_fusion
  198.7 0.1 copy.39
  198.8 5.1 %multiply_reduce_fusion.1 = f32[2,896]{1,0:T(2,128)S(1)} fusion(bf16[2,896,2368]{1,2,0:T(8,128)(2,1)} %param.8), kind=kLoop, calls=%fused_computation.23 | loop fusion | flops 12728576 | bytes 8494080 | tf_op jit(solution)/shard_map/reduce_sum | solution.py:48
  203.9 0.1 reduce_sum.53
  204.0 0.1 reduce_sum.54
  204.1 0.1 fusion.19
  204.2 11.1 %multiply_reduce_fusion = f32[]{:T(128)} fusion(bf16[9504,896]{1,0:T(8,128)(2,1)} %param.6), kind=kLoop, calls=%fused_computation.10 | loop fusion | flops 25546752 | bytes 17031172 | tf_op jit(solution)/shard_map/reduce_sum | solution.py:47
  215.3 0.6 fusion.20
  215.9 189.6 %psum.7 = f32[4]{0:T(128)S(1)} all-reduce(f32[4]{0:T(128)S(1)} %fusion.20), channel_id=1, replica_groups=mesh['dp'=4,'mp'=8] {'dp','mp'}, use_global_device_ids=true, to_apply=%region_4.5 | all-reduce | flops 4 | bytes 32 | tf_op jit(solution)/shard_map/psum | solution.py:58
  405.6 0.1 fusion.17
  405.7 0.0 copy-done.1
  405.7 0.1 fusion.18
  405.8 0.1 copy.43
  405.9 28.6 %fusion.14 = (bf16[1,4,1,2376,896]{4,3,2,1,0:T(8,128)(2,1)}, bf16[1,4,1,2376,896]{4,3,2,1,0:T(8,128)(2,1)}) fusion(bf16[4,2376,896]{2,1,0:T(8,128)(2,1)} %all-to-all-done, bf16[1,4,1,2376,896]{4,3,2,1,0:T(8,128)(2,1)} %param.7, f32[]{:T(128)S(1)} %bitcast.41), kind=kLoop, calls=%fused_computation.21 | loop fusion | flops 102187008 | bytes 68124672 | tf_op jit(solution)/shard_map/reshape | solution.py:67
  434.5 0.0 all-to-all-done.1
  434.5 15.0 %fusion.13 = (bf16[2,8,112,2368]{3,2,0,1:T(8,128)(2,1)}, bf16[2,8,112,2368]{3,2,0,1:T(8,128)(2,1)}) fusion(bf16[2,8,112,2368]{3,2,0,1:T(8,128)(2,1)} %all-to-all-done.1, f32[2,8]{0,1:T(8,128)S(1)} %copy.43, bf16[2,8,112,2368]{3,2,1,0:T(8,128)(2,1)} %param.9), kind=kLoop, calls=%fused_computation.19 | loop fusion | flops 50921472 | bytes 33947712 | tf_op jit(solution)/shard_map/convert_element_type | solution.py:17
  449.5 7.6 %copy.44 = bf16[2,8,112,2368]{3,2,1,0:T(8,128)(2,1)} copy(bf16[2,8,112,2368]{3,2,0,1:T(8,128)(2,1)} %get-tuple-element.23) | data formatting | bytes 16973824
  457.0 7.6 %copy.45 = bf16[2,8,112,2368]{3,2,1,0:T(8,128)(2,1)} copy(bf16[2,8,112,2368]{3,2,0,1:T(8,128)(2,1)} %get-tuple-element.22) | data formatting | bytes 16973824
  (3 shorter events, 0.0 us)
Async XLA Ops:
  0.6 191.5 %all-to-all-start = ((bf16[4,2376,896]{2,1,0:T(8,128)(2,1)}), bf16[4,2376,896]{2,1,0:T(8,128)(2,1)}, u32[]{:S(2)}, u32[]{:S(2)}) async-start(bf16[4,2376,896]{2,1,0:T(8,128)(2,1)} %bitcast.39), calls=%async_computation | async-start | bytes 34062336 | tf_op jit(solution)/shard_map/all_to_all | solution.py:46
  20.2 178.4 %copy-start = (s32[2,8,8]{2,1,0:T(8,128)S(1)}, s32[2,8,8]{2,1,0:T(8,128)}, u32[]{:S(2)}) copy-start(s32[2,8,8]{2,1,0:T(8,128)} %param.10) | copy-start | bytes 1540
  192.1 242.3 %all-to-all-start.1 = ((bf16[2,8,112,2368]{3,2,0,1:T(8,128)(2,1)}), bf16[2,8,112,2368]{3,2,0,1:T(8,128)(2,1)}, u32[]{:S(2)}, u32[]{:S(2)}) async-start(bf16[2,8,112,2368]{3,2,0,1:T(8,128)(2,1)} %copy.42), calls=%async_computation.1 | async-start | bytes 17432576 | tf_op jit(solution)/shard_map/all_to_all | solution.py:43
  198.6 207.2 %copy-start.1 = (f32[4]{0:T(128)S(1)}, f32[4]{0:T(128)}, u32[]{:S(2)}) copy-start(f32[4]{0:T(128)} %param.11) | copy-start | bytes 52
where the time goes:
time: 469 us; the launch traced here: 465 us
  blocking collectives  190 us (41%)
  waiting for transfers between devices  164 us (35%)
  other arithmetic  60.8 us (13%)
  local copies, waits for them, and re-layouts  35.6 us (8%)
  starting transfers between devices  13.5 us (3%)
    psum x1, blocking collectives, on_device(): totals = lax.psum(partial_value, ('dp', 'mp'))  190 us
    all_to_all x1, waiting for transfers between devices, on_device(): lax.all_to_all(emb_pieces, 'dp', split_axis=0, concat_axis=0, tiled=True)  164 us
    reshape x1, other arithmetic, on_device(): emb_moment.reshape(emb_mom.shape)  28.6 us
    unnamed x8, local copies, waits for them, and re-layouts  27.6 us
    convert_element_type x1, other arithmetic, lion_step(): (beta_second * moment + (1.0 - beta_second) * clipped).astype(jnp.bfloat16)  15 us
    reduce_sum x1, other arithmetic, on_device(): emb_squares = jnp.sum(jnp.square(emb_grad.astype(jnp.float32)))  11.1 us
  transfers between devices with their start and end apart: 2, of which 1 were waited for; matrix products, arithmetic and copies ran while one was open for 14% of the time, Pallas kernels for 0%

commit v1 on v0

--- a/solution.py
+++ b/solution.py
@@ -1,21 +1,132 @@
+import functools
+
 import jax
 import jax.numpy as jnp
 from jax import lax
+from jax.experimental import pallas as pl
+from jax.experimental.pallas import tpu as pltpu
 from jax.sharding import PartitionSpec as P
 
 beta_first = 0.9
 beta_second = 0.99
 temper = 0.05
 epsilon = 1e-06
-
-
-def lion_step(clipped, moment):
+vmem_bytes = 40 * 1024 * 1024
+
+
+def partner_tables(count):
+    if count & (count - 1) == 0:
+        return (lambda i, k: i ^ k), (lambda i, k: i ^ k)
+    return (lambda i, k: (i + k) % count), (lambda i, k: (i + count - k) % count)
+
+
+def lion_block(grad, moment, factor):
+    grad = grad.astype(jnp.float32)
     moment = moment.astype(jnp.float32)
-    update = jnp.tanh((beta_first * moment + (1.0 - beta_first) * clipped) / temper).astype(
-        jnp.bfloat16
-    )
-    new_moment = (beta_second * moment + (1.0 - beta_second) * clipped).astype(jnp.bfloat16)
-    return (update, new_moment)
+    update = jnp.tanh(
+        moment * (beta_first / temper) + grad * (factor * ((1.0 - beta_first) / temper))
+    )
+    new_moment = moment * beta_second + grad * (factor * (1.0 - beta_second))
+    return update.astype(jnp.bfloat16), new_moment.astype(jnp.bfloat16)
+
+
+def emb_body(count, aliased, sources, factors, *refs):
+    pieces = refs[:count]
+    moment = refs[count]
+    update_out, moment_out = refs[count + 1 + aliased :]
+    k = pl.program_id(0)
+    for j in range(count):
+
+        @pl.when(k == j)
+        def _():
+            update, new_moment = lion_block(pieces[j][...].reshape(moment.shape), moment[...], factors[0])
+            update_out[...] = update
+            moment_out[...] = new_moment
+
+
+def emb_step(sources, factors, own, pieces, mom, start, rows, block, outs):
+    count = mom.shape[0]
+    features = mom.shape[2]
+    blocks = pl.cdiv(rows, block)
+    first = start // block
+
+    def piece_map(j):
+        def index(k, r, s, f):
+            return (jnp.where(k < j, 0, jnp.where(k > j, blocks - 1, r)), 0)
+
+        return index
+
+    def own_map(k, r, s, f):
+        return (s[0], first + jnp.where(k > 0, blocks - 1, r), 0)
+
+    def mom_map(k, r, s, f):
+        return (s[k], first + r, 0)
+
+    whole = pl.BlockSpec((1, block, features), mom_map)
+    in_specs = (
+        [pl.BlockSpec((1, block, features), own_map)]
+        + [pl.BlockSpec((block, features), piece_map(j)) for j in range(1, count)]
+        + [whole]
+        + [pl.BlockSpec(memory_space=pl.ANY)] * len(outs)
+    )
+    shape = jax.ShapeDtypeStruct(mom.shape, jnp.bfloat16)
+    base = 2 + count + 1
+    size = count * rows * features
+    return pl.pallas_call(
+        functools.partial(emb_body, count, len(outs)),
+        out_shape=(shape, shape),
+        grid_spec=pltpu.PrefetchScalarGridSpec(
+            num_scalar_prefetch=2,
+            grid=(count, blocks),
+            in_specs=in_specs,
+            out_specs=[whole, whole],
+        ),
+        input_output_aliases={base + i: i for i in range(len(outs))},
+        compiler_params=pltpu.CompilerParams(vmem_limit_bytes=vmem_bytes),
+        cost_estimate=pl.CostEstimate(flops=8 * size, bytes_accessed=8 * size, transcendentals=size),
+    )(sources, factors, own, *pieces, mom, *outs)
+
+
+def blk_body(count, matrix, aliased, sources, factors, *refs):
+    pieces = refs[:count]
+    moment = refs[count]
+    update_out, moment_out = refs[count + 1 + aliased :]
+    k = pl.program_id(0)
+    factor = factors[matrix, sources[k]]
+    for j in range(count):
+
+        @pl.when(k == j)
+        def _():
+            update, new_moment = lion_block(pieces[j][...].reshape(moment.shape), moment[...], factor)
+            update_out[...] = update
+            moment_out[...] = new_moment
+
+
+def blk_step(sources, factors, pieces, mom, matrix, outs):
+    count = mom.shape[1]
+    rows, columns = mom.shape[2:]
+    whole = pl.BlockSpec((1, 1, rows, columns), lambda k, s, f: (matrix, s[k], 0, 0))
+    in_specs = (
+        [pl.BlockSpec((rows, columns), lambda k, s, f: (0, 0))] * count
+        + [whole]
+        + [pl.BlockSpec(memory_space=pl.ANY)] * len(outs)
+    )
+    shape = jax.ShapeDtypeStruct(mom.shape, jnp.bfloat16)
+    base = 2 + count + 1
+    size = count * rows * columns
+    return pl.pallas_call(
+        functools.partial(blk_body, count, matrix, len(outs)),
+        out_shape=(shape, shape),
+        grid_spec=pltpu.PrefetchScalarGridSpec(
+            num_scalar_prefetch=2,
+            grid=(count,),
+            in_specs=in_specs,
+            out_specs=[whole, whole],
+        ),
+        input_output_aliases={base + i: i for i in range(len(outs))},
+        compiler_params=pltpu.CompilerParams(vmem_limit_bytes=vmem_bytes),
+        cost_estimate=pl.CostEstimate(flops=8 * size, bytes_accessed=8 * size, transcendentals=size),
+    )(sources, factors, *pieces, mom, *outs)
 
 
 def on_device(emb_grad, emb_mom, blk_grad, blk_mom, tile_group, clip_rms):
@@ -39,11 +150,47 @@
     )
     owner_block = dp_index * row_blocks + mp_index * owner_rows // block_height
     owner_ids = lax.dynamic_index_in_dim(onehot, owner_block, axis=1, keepdims=False)
-    grad_pieces = blk_grad.reshape(matrices, mp_count, owner_rows, block_cols)
-    blk_owner = lax.all_to_all(grad_pieces, "mp", split_axis=1, concat_axis=1, tiled=True)
+
+    emb_to, emb_from = partner_tables(dp_count)
+    blk_to, blk_from = partner_tables(mp_count)
     emb_pieces = emb_grad.reshape(dp_count, own_rows, feature_block)
     mom_local = emb_mom.reshape(dp_count, own_rows, feature_block)
-    emb_owner = lax.all_to_all(emb_pieces, "dp", split_axis=0, concat_axis=0, tiled=True)
+    block = 256 if own_rows > 1024 else 128
+    cut = (own_rows * 3 // 4) // block * block
+    spans = ((0, cut), (cut, own_rows - cut))
+
+    def emb_send(start, rows, tie=None):
+        got = []
+        for k in range(1, dp_count):
+            piece = lax.dynamic_slice(
+                emb_pieces, (emb_to(dp_index, k), start, 0), (1, rows, feature_block)
+            )[0]
+            if tie is not None:
+                piece, _ = lax.optimization_barrier((piece, tie[k - 1]))
+            pairs = [(i, emb_to(i, k)) for i in range(dp_count)]
+            got.append(lax.ppermute(piece, "dp", pairs))
+        return got
+
+    blk_pieces = blk_grad.reshape(matrices, mp_count, owner_rows, block_cols)
+
+    def blk_send(matrix, tie=None):
+        got = []
+        for k in range(mp_count):
+            piece = lax.dynamic_index_in_dim(blk_pieces[matrix], blk_to(mp_index, k), axis=0, keepdims=False)
+            if k > 0:
+                if tie is not None:
+                    piece, _ = lax.optimization_barrier((piece, tie[k]))
+                pairs = [(i, blk_to(i, k)) for i in range(mp_count)]
+                piece = lax.ppermute(piece, "mp", pairs)
+            got.append(piece)
+        return got
+
+    emb_got = [emb_send(*spans[0])]
+    blk_got = [blk_send(0)]
+    emb_got.append(emb_send(*spans[1], tie=emb_got[0]))
+    for matrix in range(1, matrices):
+        blk_got.append(blk_send(matrix, tie=blk_got[-1]))
+
     emb_squares = jnp.sum(jnp.square(emb_grad.astype(jnp.float32)))
     block_squares = jnp.sum(
         jnp.square(blk_grad.astype(jnp.float32)).reshape(
@@ -59,14 +206,22 @@
     root_mean = jnp.sqrt(totals / jnp.maximum(counts, 1.0))
     factor = jnp.minimum(1.0, clip_rms / (root_mean + epsilon))
     owner_factor = jnp.sum(owner_ids * factor, axis=-1)
-    clipped = blk_owner.astype(jnp.float32) * owner_factor[:, :, None, None]
-    blk_update, blk_moment = lion_step(clipped, blk_mom)
-    emb_update, emb_moment = lion_step(emb_owner.astype(jnp.float32) * factor[0], mom_local)
+
+    emb_sources = jnp.stack([emb_from(dp_index, k) for k in range(dp_count)]).astype(jnp.int32)
+    blk_sources = jnp.stack([blk_from(mp_index, k) for k in range(mp_count)]).astype(jnp.int32)
+    emb_outs = ()
+    for (start, rows), got in zip(spans, emb_got):
+        emb_outs = emb_step(
+            emb_sources, factor, emb_pieces, got, mom_local, start, rows, block, emb_outs
+        )
+    blk_outs = ()
+    for matrix in range(matrices):
+        blk_outs = blk_step(blk_sources, owner_factor, blk_got[matrix], blk_mom, matrix, blk_outs)
     return (
-        emb_update.reshape(emb_mom.shape),
-        emb_moment.reshape(emb_mom.shape),
-        blk_update,
-        blk_moment,
+        emb_outs[0].reshape(emb_mom.shape),
+        emb_outs[1].reshape(emb_mom.shape),
+        blk_outs[0],
+        blk_outs[1],
     )
 
 

time: 469 us -> 361 us (0.77)
  blocking collectives: 190 us -> 68.9 us
  waiting for transfers between devices: 164 us -> 73.4 us
  starting transfers between devices: 13.5 us -> 84.2 us
  Pallas kernels: 0 us -> 57.9 us
  other arithmetic: 60.8 us -> 14.9 us
  local copies, waits for them, and re-layouts: 35.6 us -> 58.7 us
    all_to_all x2 -> x0, waiting for transfers between devices: 164 us -> none  [the longest x1 164 us: on_device(): lax.all_to_all(emb_pieces, 'dp', split_axis=0, concat_axis=0, tiled=True)]
    psum x1, blocking collectives: 190 us -> 68.9 us  [on_device(): totals = lax.psum(partial_value, ('dp', 'mp'))]
    ppermute x0 -> x20, starting transfers between devices: none -> 84.2 us  [the longest x14 80.3 us: blk_send(): piece = lax.ppermute(piece, 'mp', pairs)]
    ppermute x0 -> x20, waiting for transfers between devices: none -> 73.4 us  [the longest x14 70.5 us: blk_send(): piece = lax.ppermute(piece, 'mp', pairs)]
    pallas_call x0 -> x4, Pallas kernels: none -> 57.9 us  [the longest x2 41.9 us: emb_step(): pl.pallas_call(functools.partial(emb_body, count, len(outs)), out_shape=(...]
    reshape x1 -> x0, other arithmetic: 28.6 us -> none  [on_device(): emb_moment.reshape(emb_mom.shape)]
    squeeze x0 -> x4, local copies, waits for them, and re-layouts: none -> 19.5 us  [the longest x2 11.6 us: emb_send(): lax.dynamic_slice(emb_pieces, (emb_to(dp_index, k), start, 0), (1, rows,...]
    convert_element_type x1 -> x0, other arithmetic: 15 us -> none  [lion_step(): (beta_second * moment + (1.0 - beta_second) * clipped).astype(jnp.bfloat16)]
  transfers between devices with their start and end apart: 2 -> 20, of which waited for: 1 -> 9; matrix products, arithmetic and copies ran while one was open for 14% -> 13% of each run, Pallas kernels for 0% -> 11%
where the time goes in v1:
time: 361 us; the launch traced here: 359 us
  starting transfers between devices  84.2 us (23%)
  waiting for transfers between devices  73.4 us (20%)
  blocking collectives  68.9 us (19%)
  local copies, waits for them, and re-layouts  58.7 us (16%)
  Pallas kernels  57.9 us (16%)
  other arithmetic  14.9 us (4%)
    ppermute x14, starting transfers between devices, blk_send(): piece = lax.ppermute(piece, 'mp', pairs)  80.3 us
    ppermute x14, waiting for transfers between devices, blk_send(): piece = lax.ppermute(piece, 'mp', pairs)  70.5 us
    psum x1, blocking collectives, on_device(): totals = lax.psum(partial_value, ('dp', 'mp'))  68.9 us
    pallas_call x2, Pallas kernels, emb_step(): pl.pallas_call(functools.partial(emb_body, count, len(outs)), out_shape=(...  41.9 us
    unnamed x59, local copies, waits for them, and re-layouts  32.8 us
    pallas_call x2, Pallas kernels, blk_step(): pl.pallas_call(functools.partial(blk_body, count, matrix, len(outs)), out...  16 us
    reduce_sum x1, other arithmetic, on_device(): emb_squares = jnp.sum(jnp.square(emb_grad.astype(jnp.float32)))  12.1 us
    squeeze x2, local copies, waits for them, and re-layouts, emb_send(): lax.dynamic_slice(emb_pieces, (emb_to(dp_index, k), start, 0), (1, rows,...  11.6 us
  transfers between devices with their start and end apart: 20, of which 9 were waited for; matrix products, arithmetic and copies ran while one was open for 13% of the time, Pallas kernels for 11%

profile of v1, /device:TPU:9, one launch (start us, length us, event | category | flops | bytes accessed | tf_op | source)
XLA Modules:
  0.0 358.8 jit_solution(8760453042743947356)
XLA Ops:
  0.7 7.1 %dynamic-slice_bitcast_fusion = (bf16[1536,896]{1,0:T(8,128)(2,1)}, bf16[1536,896]{1,0:T(8,128)(2,1)}, bf16[1536,896]{1,0:T(8,128)(2,1)}) fusion(bf16[4,2376,896]{2,1,0:T(8,128)(2,1)} %bitcast.76, s32[]{:T(128)S(6)} %select_n.69, s32[]{:T(128)S(6)} %select_n.68, s32[]{:T(128)S(6)} %select_n.67), kind=kLoop, calls=%fused_computation.2 | loop fusion | bytes 16515084 | tf_op jit(solution)/shard_map/squeeze | solution.py:165
  10.4 5.9 %fusion.11 = (bf16[1,896,2368]{1,2,0:T(8,128)(2,1)}, bf16[1,896,2368]{1,2,0:T(8,128)(2,1)}) fusion(bf16[2,896,2368]{1,2,0:T(8,128)(2,1)} %param.8), kind=kLoop, calls=%fused_computation.43 | loop fusion | bytes 16973824 | tf_op jit(solution)/shard_map/slice | solution.py:179
  16.3 7.1 %copy.47 = bf16[1,896,2368]{2,1,0:T(8,128)(2,1)} copy(bf16[1,896,2368]{1,2,0:T(8,128)(2,1)} %get-tuple-element.58) | data formatting | bytes 8486912
  23.4 4.0 %dynamic-slice_bitcast_fusion.6 = (bf16[112,2368]{1,0:T(8,128)(2,1)S(1)}, bf16[112,2368]{1,0:T(8,128)(2,1)}, bf16[112,2368]{1,0:T(8,128)(2,1)}, bf16[112,2368]{1...) fusion(bf16[8,112,2368]{2,1,0:T(8,128)(2,1)} %bitcast.84, ...), kind=kLoop, calls=%fused_computation.8 | loop fusion | bytes 8486944 | tf_op jit(solution)/shard_map/jit(dynamic_index_in_dim)/squeeze | solution.py:179
  27.4 1.5 collective-permute-start.6
  28.9 1.6 collective-permute-done.6.refs_1_
  31.4 7.1 %copy.46 = bf16[1,896,2368]{2,1,0:T(8,128)(2,1)} copy(bf16[1,896,2368]{1,2,0:T(8,128)(2,1)} %get-tuple-element.59) | data formatting | bytes 8486912
  38.4 3.9 %dynamic-slice_bitcast_fusion.8 = (bf16[112,2368]{1,0:T(8,128)(2,1)}, bf16[112,2368]{1,0:T(8,128)(2,1)}, bf16[112,2368]{1,0:T(8,128)(2,1)}, bf16[112,2368]{1,0:T...) fusion(bf16[8,112,2368]{2,1,0:T(8,128)(2,1)} %bitcast.85, ...), kind=kLoop, calls=%fused_computation.10 | loop fusion | bytes 8486944 | tf_op jit(solution)/shard_map/jit(dynamic_index_in_dim)/squeeze | solution.py:179
  43.2 2.3 collective-permute-start.12
  45.5 17.1 %collective-permute-done.10.refs_3_ = bf16[112,2368]{1,0:T(8,128)(2,1)} collective-permute-done((bf16[112,2368]{1,0:T(8,128)(2,1)}, bf16[112,2368]{1,0:T(8,128)(2,1)}, u32[]{:S(2)}, u32[]{:S(2)}) %collective-permute-start.10) | collective-permute-done | bytes 530464 | tf_op jit(solution)/shard_map/ppermute | solution.py:184
  62.6 3.0 collective-permute-start.14
  65.7 2.9 collective-permute-done.refs_1_
  68.6 1.3 collective-permute-start.16
  69.9 61.6 %collective-permute-start.18 = (bf16[112,2368]{1,0:T(8,128)(2,1)S(1)}, bf16[112,2368]{1,0:T(8,128)(2,1)S(1)}, u32[]{:S(2)}, u32[]{:S(2)}) collective-permute-start(bf16[112,2368]{1,0:T(8,128)(2,1)S(1)} %copy-done.19), channel_id=1, source_target_pairs={{0,7},{1,6},{2,5},{3,4},{4,3},{5,2},{6,1},{7,0},{8,15},{9,14},{10,... | collective-permute-start | bytes 1591304 | tf_op jit(solution)/shard_map/ppermute | solution.py:184
  131.5 12.1 %multiply_reduce_fusion = f32[]{:T(128)} fusion(bf16[9504,896]{1,0:T(8,128)(2,1)} %param.6), kind=kLoop, calls=%fused_computation | loop fusion | flops 25546752 | bytes 17031172 | tf_op jit(solution)/shard_map/reduce_sum | solution.py:194
  143.6 4.5 %dynamic-slice_bitcast_fusion.3 = (bf16[840,896]{1,0:T(8,128)(2,1)}, bf16[840,896]{1,0:T(8,128)(2,1)}, bf16[840,896]{1,0:T(8,128)(2,1)}) fusion(bf16[4,2376,896]{2,1,0:T(8,128)(2,1)} %bitcast.77, s32[]{:T(128)S(6)} %select_n.69, s32[]{:T(128)S(6)} %select_n.68, s32[]{:T(128)S(6)} %select_n.67), kind=kLoop, calls=%fused_computation.5 | loop fusion | bytes 9031692 | tf_op jit(solution)/shard_map/squeeze | solution.py:165
  149.0 2.2 collective-permute-start.9
  153.2 3.0 collective-permute-done.18.refs_7_
  159.2 1.7 multiply_reduce_fusion.1
  160.9 2.7 collective-permute-done.9.refs_2_
  164.8 16.1 %collective-permute-done.11.refs_3_ = bf16[112,2368]{1,0:T(8,128)(2,1)S(1)} collective-permute-done((bf16[112,2368]{1,0:T(8,128)(2,1)S(1)}, bf16[112,2368]{1,0:T(8,128)(2,1)S(1)}, u32[]{:S(2)}, u32[]{:S(2)}) %collective-permute-start.11) | collective-permute-done | bytes 530464 | tf_op jit(solution)/shard_map/ppermute | solution.py:184
  181.7 4.2 %collective-permute-start.15 = (bf16[112,2368]{1,0:T(8,128)(2,1)}, bf16[112,2368]{1,0:T(8,128)(2,1)}, u32[]{:S(2)}, u32[]{:S(2)}) collective-permute-start(bf16[112,2368]{1,0:T(8,128)(2,1)} %get-tuple-element.33), channel_id=1, source_target_pairs={{0,5},{1,4},{2,7},{3,6},{4,1},{5,0},{6,3},{7,2},{8,13},{9,12},{10,... | collective-permute-start | bytes 1591304 | tf_op jit(solution)/shard_map/ppermute | solution.py:184
  187.0 68.9 %psum.7 = f32[4]{0:T(128)S(1)} all-reduce(f32[4]{0:T(128)S(1)} %fusion.6), channel_id=1, replica_groups=mesh['dp'=4,'mp'=8] {'dp','mp'}, use_global_device_ids=true, to_apply=%region_4.5 | all-reduce | flops 4 | bytes 32 | tf_op jit(solution)/shard_map/psum | solution.py:205
  257.2 2.0 collective-permute-start.19
  259.5 3.5 copy-done
  268.3 8.0 %shard_map.95 = (bf16[2,8,112,2368]{3,2,1,0:T(8,128)(2,1)}, bf16[2,8,112,2368]{3,2,1,0:T(8,128)(2,1)}) custom-call(s32[8]{0:T(128)S(1)} %stack.55.sources, f32[2,8]{1,0:T(2,128)S(1)} %fusion.4.factors, bf16[112,2368]{1,0:T(8,128)(2,1)S(1)} %get-tuple-element.60.refs_0_, bf16[112,2368]{1,0:T(8,128)(2,1)S(1)} %copy-done.4, ...), custom_call_target="tpu_custom_call" | custom-call | flops 16973824 | bytes 16973824 | tf_op jit(solution)/shard_map/pallas_call | solution.py:117
  276.3 17.4 %collective-permute-done.17.refs_6_ = bf16[112,2368]{1,0:T(8,128)(2,1)S(1)} collective-permute-done((bf16[112,2368]{1,0:T(8,128)(2,1)}, bf16[112,2368]{1,0:T(8,128)(2,1)S(1)}, u32[]{:S(2)}, u32[]{:S(2)}) %collective-permute-start.17) | collective-permute-done | bytes 530464 | tf_op jit(solution)/shard_map/ppermute | solution.py:184
  293.7 11.7 %collective-permute-done.19.refs_7_ = bf16[112,2368]{1,0:T(8,128)(2,1)S(1)} collective-permute-done((bf16[112,2368]{1,0:T(8,128)(2,1)}, bf16[112,2368]{1,0:T(8,128)(2,1)S(1)}, u32[]{:S(2)}, u32[]{:S(2)}) %collective-permute-start.19) | collective-permute-done | bytes 530464 | tf_op jit(solution)/shard_map/ppermute | solution.py:184
  305.4 3.5 copy-done.1
  308.9 8.0 %shard_map.96 = (bf16[2,8,112,2368]{3,2,1,0:T(8,128)(2,1)}, bf16[2,8,112,2368]{3,2,1,0:T(8,128)(2,1)}) custom-call(s32[8]{0:T(128)S(1)} %stack.55.sources, f32[2,8]{1,0:T(2,128)S(1)} %fusion.4.factors, bf16[112,2368]{1,0:T(8,128)(2,1)S(1)} %copy-done.2, bf16[112,2368]{1,0:T(8,128)(2,1)S(1)} %copy-done.14, ...), custom_call_target="tpu_custom_call", output_to_operand_aliasing={{0}: (11, {}), {1}: (12, {})} | custom-call | flops 16973824 | bytes 16973824 | tf_op jit(solution)/shard_map/pallas_call | solution.py:117
  316.9 25.0 %shard_map.93 = (bf16[4,2376,896]{2,1,0:T(8,128)(2,1)}, bf16[4,2376,896]{2,1,0:T(8,128)(2,1)}) custom-call(s32[4]{0:T(128)S(1)} %pad_add_fusion.sources, f32[4]{0:T(128)S(1)} %fusion.10.factors, bf16[4,2376,896]{2,1,0:T(8,128)(2,1)} %bitcast.78, bf16[1536,896]{1,0:T(8,128)(2,1)S(1)} %collective-permute-done.refs_1_, ...), custom_call_target="tpu_custom_call" | custom-call | flops 44040192 | bytes 44040192 | tf_op jit(solution)/shard_map/pallas_call | solution.py:75
  341.9 16.9 %shard_map.94 = (bf16[4,2376,896]{2,1,0:T(8,128)(2,1)}, bf16[4,2376,896]{2,1,0:T(8,128)(2,1)}) custom-call(s32[4]{0:T(128)S(1)} %pad_add_fusion.sources, f32[4]{0:T(128)S(1)} %fusion.10.factors, bf16[4,2376,896]{2,1,0:T(8,128)(2,1)} %bitcast.79, bf16[840,896]{1,0:T(8,128)(2,1)} %collective-permute-done.1.refs_1_, ...), custom_call_target="tpu_custom_call", output_to_operand_aliasing={{0}: (7, {}), {1}: (8, {})} | custom-call | flops 24084480 | bytes 24084480 | tf_op jit(solution)/shard_map/pallas_call | solution.py:75
  (92 shorter events, 20.0 us)
Async XLA Ops:
  7.7 60.9 %collective-permute-start = (bf16[1536,896]{1,0:T(8,128)(2,1)}, bf16[1536,896]{1,0:T(8,128)(2,1)S(1)}, u32[]{:S(2)}, u32[]{:S(2)}) collective-permute-start(bf16[1536,896]{1,0:T(8,128)(2,1)} %get-tuple-element.54), channel_id=1, source_target_pairs={{0,8},{8,0},{16,24},{24,16},{1,9},{9,1},{17,25},{25,17},{2,10},{10... | collective-permute-start | bytes 8257544 | tf_op jit(solution)/shard_map/ppermute | solution.py:171
  8.9 61.0 %collective-permute-start.2 = (bf16[1536,896]{1,0:T(8,128)(2,1)}, bf16[1536,896]{1,0:T(8,128)(2,1)}, u32[]{:S(2)}, u32[]{:S(2)}) collective-permute-start(bf16[1536,896]{1,0:T(8,128)(2,1)} %get-tuple-element.53), channel_id=1, source_target_pairs={{0,16},{8,24},{16,0},{24,8},{1,17},{9,25},{17,1},{25,9},{2,18},{10... | collective-permute-start | bytes 8257544 | tf_op jit(solution)/shard_map/ppermute | solution.py:171
  10.2 121.3 %collective-permute-start.4 = (bf16[1536,896]{1,0:T(8,128)(2,1)}, bf16[1536,896]{1,0:T(8,128)(2,1)}, u32[]{:S(2)}, u32[]{:S(2)}) collective-permute-start(bf16[1536,896]{1,0:T(8,128)(2,1)} %get-tuple-element.52), channel_id=1, source_target_pairs={{0,24},{8,16},{16,8},{24,0},{1,25},{9,17},{17,9},{25,1},{2,26},{10... | collective-permute-start | bytes 8257544 | tf_op jit(solution)/shard_map/ppermute | solution.py:171
  27.4 3.1 collective-permute-start.6
  28.9 14.3 %collective-permute-start.8 = (bf16[112,2368]{1,0:T(8,128)(2,1)}, bf16[112,2368]{1,0:T(8,128)(2,1)}, u32[]{:S(2)}, u32[]{:S(2)}) collective-permute-start(bf16[112,2368]{1,0:T(8,128)(2,1)} %get-tuple-element.66), channel_id=1, source_target_pairs={{0,2},{1,3},{2,0},{3,1},{4,6},{5,7},{6,4},{7,5},{8,10},{9,11},{10,... | collective-permute-start | bytes 1591304 | tf_op jit(solution)/shard_map/ppermute | solution.py:184
  31.3 31.4 %collective-permute-start.10 = (bf16[112,2368]{1,0:T(8,128)(2,1)}, bf16[112,2368]{1,0:T(8,128)(2,1)}, u32[]{:S(2)}, u32[]{:S(2)}) collective-permute-start(bf16[112,2368]{1,0:T(8,128)(2,1)} %get-tuple-element.65), channel_id=1, source_target_pairs={{0,3},{1,2},{2,1},{3,0},{4,7},{5,6},{6,5},{7,4},{8,11},{9,10},{10,... | collective-permute-start | bytes 1591304 | tf_op jit(solution)/shard_map/ppermute | solution.py:184
  38.4 24.2 %copy-start.21 = (bf16[112,2368]{1,0:T(8,128)(2,1)S(1)}, bf16[112,2368]{1,0:T(8,128)(2,1)}, u32[]{:S(2)}) copy-start(bf16[112,2368]{1,0:T(8,128)(2,1)} %get-tuple-element.63) | copy-start | bytes 1591300
  38.4 30.1 %copy-start.20 = (bf16[112,2368]{1,0:T(8,128)(2,1)S(1)}, bf16[112,2368]{1,0:T(8,128)(2,1)}, u32[]{:S(2)}) copy-start(bf16[112,2368]{1,0:T(8,128)(2,1)} %get-tuple-element.62) | copy-start | bytes 1591300
  38.4 31.4 %copy-start.19 = (bf16[112,2368]{1,0:T(8,128)(2,1)S(1)}, bf16[112,2368]{1,0:T(8,128)(2,1)}, u32[]{:S(2)}) copy-start(bf16[112,2368]{1,0:T(8,128)(2,1)} %get-tuple-element.61) | copy-start | bytes 1591300
  43.2 105.0 %collective-permute-start.12 = (bf16[112,2368]{1,0:T(8,128)(2,1)S(1)}, bf16[112,2368]{1,0:T(8,128)(2,1)S(1)}, u32[]{:S(2)}, u32[]{:S(2)}) collective-permute-start(bf16[112,2368]{1,0:T(8,128)(2,1)S(1)} %copy-done.22), channel_id=1, source_target_pairs={{0,4},{1,5},{2,6},{3,7},{4,0},{5,1},{6,2},{7,3},{8,12},{9,13},{10,... | collective-permute-start | bytes 1591304 | tf_op jit(solution)/shard_map/ppermute | solution.py:184
  62.6 88.6 %collective-permute-start.14 = (bf16[112,2368]{1,0:T(8,128)(2,1)S(1)}, bf16[112,2368]{1,0:T(8,128)(2,1)S(1)}, u32[]{:S(2)}, u32[]{:S(2)}) collective-permute-start(bf16[112,2368]{1,0:T(8,128)(2,1)S(1)} %copy-done.21), channel_id=1, source_target_pairs={{0,5},{1,4},{2,7},{3,6},{4,1},{5,0},{6,3},{7,2},{8,13},{9,12},{10,... | collective-permute-start | bytes 1591304 | tf_op jit(solution)/shard_map/ppermute | solution.py:184
  68.6 83.8 %collective-permute-start.16 = (bf16[112,2368]{1,0:T(8,128)(2,1)S(1)}, bf16[112,2368]{1,0:T(8,128)(2,1)S(1)}, u32[]{:S(2)}, u32[]{:S(2)}) collective-permute-start(bf16[112,2368]{1,0:T(8,128)(2,1)S(1)} %copy-done.20), channel_id=1, source_target_pairs={{0,6},{1,7},{2,4},{3,5},{4,2},{5,3},{6,0},{7,1},{8,14},{9,15},{10,... | collective-permute-start | bytes 1591304 | tf_op jit(solution)/shard_map/ppermute | solution.py:184
  69.9 86.4 %collective-permute-start.18 = (bf16[112,2368]{1,0:T(8,128)(2,1)S(1)}, bf16[112,2368]{1,0:T(8,128)(2,1)S(1)}, u32[]{:S(2)}, u32[]{:S(2)}) collective-permute-start(bf16[112,2368]{1,0:T(8,128)(2,1)S(1)} %copy-done.19), channel_id=1, source_target_pairs={{0,7},{1,6},{2,5},{3,4},{4,3},{5,2},{6,1},{7,0},{8,15},{9,14},{10,... | collective-permute-start | bytes 1591304 | tf_op jit(solution)/shard_map/ppermute | solution.py:184
  131.5 26.8 %collective-permute-start.7 = (bf16[112,2368]{1,0:T(8,128)(2,1)S(1)}, bf16[112,2368]{1,0:T(8,128)(2,1)S(1)}, u32[]{:S(2)}, u32[]{:S(2)}) collective-permute-start(bf16[112,2368]{1,0:T(8,128)(2,1)S(1)} %get-tuple-element.29), channel_id=1, source_target_pairs={{0,1},{1,0},{2,3},{3,2},{4,5},{5,4},{6,7},{7,6},{8,9},{9,8},{10,11... | collective-permute-start | bytes 1591304 | tf_op jit(solution)/shard_map/ppermute | solution.py:184
  131.5 27.6 %slice-start = ((s8[8486912]{0:T(1024)(128)(4,1)}), s8[4194304]{0:T(1024)(128)(4,1)S(1)}, s32[]{:S(2)}) async-start(s8[8486912]{0:T(1024)(128)(4,1)} %bitcast.82), calls=%async_computation | async-start | bytes 8388608
  131.5 27.6 %slice-start.1 = ((s8[8486912]{0:T(1024)(128)(4,1)}), s8[4194304]{0:T(1024)(128)(4,1)S(1)}, s32[]{:S(2)}) async-start(s8[8486912]{0:T(1024)(128)(4,1)} %bitcast.82), calls=%async_computation.1 | async-start | bytes 8388608
  143.6 15.5 %slice-start.2 = ((s8[8486912]{0:T(1024)(128)(4,1)}), s8[98304]{0:T(1024)(128)(4,1)S(1)}, s32[]{:S(2)}) async-start(s8[8486912]{0:T(1024)(128)(4,1)} %bitcast.82), calls=%async_computation.2 | async-start | bytes 196608
  148.2 12.7 %copy-start.23 = (s32[2,8,8]{2,1,0:T(8,128)S(1)}, s32[2,8,8]{2,1,0:T(8,128)}, u32[]{:S(2)}) copy-start(s32[2,8,8]{2,1,0:T(8,128)} %param.10) | copy-start | bytes 1540
  148.2 111.2 %copy-start.24 = (f32[4]{0:T(128)S(1)}, f32[4]{0:T(128)}, u32[]{:S(2)}) copy-start(f32[4]{0:T(128)} %param.11) | copy-start | bytes 52
  149.0 14.6 %collective-permute-start.9 = (bf16[112,2368]{1,0:T(8,128)(2,1)S(1)}, bf16[112,2368]{1,0:T(8,128)(2,1)S(1)}, u32[]{:S(2)}, u32[]{:S(2)}) collective-permute-start(bf16[112,2368]{1,0:T(8,128)(2,1)S(1)} %get-tuple-element.30), channel_id=1, source_target_pairs={{0,2},{1,3},{2,0},{3,1},{4,6},{5,7},{6,4},{7,5},{8,10},{9,11},{10,... | collective-permute-start | bytes 1591304 | tf_op jit(solution)/shard_map/ppermute | solution.py:184
  152.0 28.9 %collective-permute-start.11 = (bf16[112,2368]{1,0:T(8,128)(2,1)S(1)}, bf16[112,2368]{1,0:T(8,128)(2,1)S(1)}, u32[]{:S(2)}, u32[]{:S(2)}) collective-permute-start(bf16[112,2368]{1,0:T(8,128)(2,1)S(1)} %get-tuple-element.31), channel_id=1, source_target_pairs={{0,3},{1,2},{2,1},{3,0},{4,7},{5,6},{6,5},{7,4},{8,11},{9,10},{10,... | collective-permute-start | bytes 1591304 | tf_op jit(solution)/shard_map/ppermute | solution.py:184
  153.2 188.7 %collective-permute-start.1 = (bf16[840,896]{1,0:T(8,128)(2,1)}, bf16[840,896]{1,0:T(8,128)(2,1)}, u32[]{:S(2)}, u32[]{:S(2)}) collective-permute-start(bf16[840,896]{1,0:T(8,128)(2,1)} %get-tuple-element.22), channel_id=1, source_target_pairs={{0,8},{8,0},{16,24},{24,16},{1,9},{9,1},{17,25},{25,17},{2,10},{10... | collective-permute-start | bytes 4515848 | tf_op jit(solution)/shard_map/ppermute | solution.py:171
  157.1 184.8 %collective-permute-start.3 = (bf16[840,896]{1,0:T(8,128)(2,1)}, bf16[840,896]{1,0:T(8,128)(2,1)}, u32[]{:S(2)}, u32[]{:S(2)}) collective-permute-start(bf16[840,896]{1,0:T(8,128)(2,1)} %get-tuple-element.23), channel_id=1, source_target_pairs={{0,16},{8,24},{16,0},{24,8},{1,17},{9,25},{17,1},{25,9},{2,18},{10... | collective-permute-start | bytes 4515848 | tf_op jit(solution)/shard_map/ppermute | solution.py:171
  159.1 182.8 %collective-permute-start.5 = (bf16[840,896]{1,0:T(8,128)(2,1)}, bf16[840,896]{1,0:T(8,128)(2,1)}, u32[]{:S(2)}, u32[]{:S(2)}) collective-permute-start(bf16[840,896]{1,0:T(8,128)(2,1)} %get-tuple-element.24), channel_id=1, source_target_pairs={{0,24},{8,16},{16,8},{24,0},{1,25},{9,17},{17,9},{25,1},{2,26},{10... | collective-permute-start | bytes 4515848 | tf_op jit(solution)/shard_map/ppermute | solution.py:171
  164.4 91.6 %collective-permute-start.13 = (bf16[112,2368]{1,0:T(8,128)(2,1)}, bf16[112,2368]{1,0:T(8,128)(2,1)}, u32[]{:S(2)}, u32[]{:S(2)}) collective-permute-start(bf16[112,2368]{1,0:T(8,128)(2,1)} %get-tuple-element.32), channel_id=1, source_target_pairs={{0,4},{1,5},{2,6},{3,7},{4,0},{5,1},{6,2},{7,3},{8,12},{9,13},{10,... | collective-permute-start | bytes 1591304 | tf_op jit(solution)/shard_map/ppermute | solution.py:184
  181.7 75.4 %collective-permute-start.15 = (bf16[112,2368]{1,0:T(8,128)(2,1)}, bf16[112,2368]{1,0:T(8,128)(2,1)}, u32[]{:S(2)}, u32[]{:S(2)}) collective-permute-start(bf16[112,2368]{1,0:T(8,128)(2,1)} %get-tuple-element.33), channel_id=1, source_target_pairs={{0,5},{1,4},{2,7},{3,6},{4,1},{5,0},{6,3},{7,2},{8,13},{9,12},{10,... | collective-permute-start | bytes 1591304 | tf_op jit(solution)/shard_map/ppermute | solution.py:184
  256.0 37.7 %collective-permute-start.17 = (bf16[112,2368]{1,0:T(8,128)(2,1)}, bf16[112,2368]{1,0:T(8,128)(2,1)S(1)}, u32[]{:S(2)}, u32[]{:S(2)}) collective-permute-start(bf16[112,2368]{1,0:T(8,128)(2,1)} %get-tuple-element.34), channel_id=1, source_target_pairs={{0,6},{1,7},{2,4},{3,5},{4,2},{5,3},{6,0},{7,1},{8,14},{9,15},{10,... | collective-permute-start | bytes 1591304 | tf_op jit(solution)/shard_map/ppermute | solution.py:184
  257.2 48.2 %collective-permute-start.19 = (bf16[112,2368]{1,0:T(8,128)(2,1)}, bf16[112,2368]{1,0:T(8,128)(2,1)S(1)}, u32[]{:S(2)}, u32[]{:S(2)}) collective-permute-start(bf16[112,2368]{1,0:T(8,128)(2,1)} %get-tuple-element.35), channel_id=1, source_target_pairs={{0,7},{1,6},{2,5},{3,4},{4,3},{5,2},{6,1},{7,0},{8,15},{9,14},{10,... | collective-permute-start | bytes 1591304 | tf_op jit(solution)/shard_map/ppermute | solution.py:184
  268.3 37.1 %copy-start.2 = (bf16[112,2368]{1,0:T(8,128)(2,1)S(1)}, bf16[112,2368]{1,0:T(8,128)(2,1)}, u32[]{:S(2)}) copy-start(bf16[112,2368]{1,0:T(8,128)(2,1)} %get-tuple-element.75.refs_0_) | copy-start | bytes 1591300
  268.3 37.1 %copy-start.14 = (bf16[112,2368]{1,0:T(8,128)(2,1)S(1)}, bf16[112,2368]{1,0:T(8,128)(2,1)}, u32[]{:S(2)}) copy-start(bf16[112,2368]{1,0:T(8,128)(2,1)} %copy-done.13) | copy-start | bytes 1591300
  268.3 37.1 %copy-start.16 = (bf16[112,2368]{1,0:T(8,128)(2,1)S(1)}, bf16[112,2368]{1,0:T(8,128)(2,1)}, u32[]{:S(2)}) copy-start(bf16[112,2368]{1,0:T(8,128)(2,1)} %copy-done.15) | copy-start | bytes 1591300
  268.3 37.1 %copy-start.18 = (bf16[112,2368]{1,0:T(8,128)(2,1)S(1)}, bf16[112,2368]{1,0:T(8,128)(2,1)}, u32[]{:S(2)}) copy-start(bf16[112,2368]{1,0:T(8,128)(2,1)} %copy-done.17) | copy-start | bytes 1591300
  (16 other events, 23.4 us)

commit v2 on v0

--- a/solution.py
+++ b/solution.py
@@ -1,21 +1,123 @@
+import functools
+
 import jax
 import jax.numpy as jnp
 from jax import lax
+from jax.experimental import pallas as pl
+from jax.experimental.pallas import tpu as pltpu
 from jax.sharding import PartitionSpec as P
 
 beta_first = 0.9
 beta_second = 0.99
 temper = 0.05
 epsilon = 1e-06
-
-
-def lion_step(clipped, moment):
+vmem_bytes = 60 * 1024 * 1024
+
+
+def partner_tables(count):
+    if count & (count - 1) == 0:
+        return (lambda i, k: i ^ k), (lambda i, k: i ^ k)
+    return (lambda i, k: (i + k) % count), (lambda i, k: (i + count - k) % count)
+
+
+def lion_rows(grad, moment, factor):
+    grad = grad.astype(jnp.float32)
     moment = moment.astype(jnp.float32)
-    update = jnp.tanh((beta_first * moment + (1.0 - beta_first) * clipped) / temper).astype(
-        jnp.bfloat16
-    )
-    new_moment = (beta_second * moment + (1.0 - beta_second) * clipped).astype(jnp.bfloat16)
-    return (update, new_moment)
+    update = jnp.tanh(
+        moment * (beta_first / temper) + grad * (factor * ((1.0 - beta_first) / temper))
+    )
+    new_moment = moment * beta_second + grad * (factor * (1.0 - beta_second))
+    return update.astype(jnp.bfloat16), new_moment.astype(jnp.bfloat16)
+
+
+def lion_block(grad, moment, update_out, moment_out, factor):
+    rows = moment.shape[0]
+    height = 16 if rows > 128 and rows % 16 == 0 else rows
+
+    @pl.loop(0, rows // height)
+    def _(i):
+        at = pl.ds(pl.multiple_of(i * height, height), height)
+        update, new_moment = lion_rows(grad[at, :], moment[at, :], factor)
+        update_out[at, :] = update
+        moment_out[at, :] = new_moment
+
+
+def emb_body(count, sources, factors, *refs):
+    own, *pieces = refs[:count]
+    pieces = [own.at[0]] + pieces
+    moment, update_out, moment_out = refs[count:]
+    k = pl.program_id(0)
+    for j in range(count):
+
+        @pl.when(k == j)
+        def _():
+            lion_block(pieces[j], moment.at[0], update_out.at[0], moment_out.at[0], factors[0])
+
+
+def emb_step(sources, factors, own, pieces, mom, block):
+    count, rows, features = mom.shape
+    blocks = pl.cdiv(rows, block)
+
+    def piece_map(j):
+        def index(k, r, s, f):
+            return (jnp.where(k < j, 0, jnp.where(k > j, blocks - 1, r)), 0)
+
+        return index
+
+    def own_map(k, r, s, f):
+        return (s[0], jnp.where(k > 0, blocks - 1, r), 0)
+
+    def mom_map(k, r, s, f):
+        return (s[k], r, 0)
+
+    whole = pl.BlockSpec((1, block, features), mom_map)
+    in_specs = (
+        [pl.BlockSpec((1, block, features), own_map)]
+        + [pl.BlockSpec((block, features), piece_map(j)) for j in range(1, count)]
+        + [whole]
+    )
+    shape = jax.ShapeDtypeStruct(mom.shape, jnp.bfloat16)
+    size = count * rows * features
+    return pl.pallas_call(
+        functools.partial(emb_body, count),
+        out_shape=(shape, shape),
+        grid_spec=pltpu.PrefetchScalarGridSpec(
+            num_scalar_prefetch=2,
+            grid=(count, blocks),
+            in_specs=in_specs,
+            out_specs=[whole, whole],
+        ),
+        compiler_params=pltpu.CompilerParams(vmem_limit_bytes=vmem_bytes),
+        cost_estimate=pl.CostEstimate(flops=8 * size, bytes_accessed=8 * size, transcendentals=size),
+    )(sources, factors, own, *pieces, mom)
+
+
+def blk_body(factors, grad, moment, update_out, moment_out):
+    factor = factors[pl.program_id(0), pl.program_id(1)]
+    lion_block(
+        grad.at[0, 0], moment.at[0, 0], update_out.at[0, 0], moment_out.at[0, 0], factor
+    )
+
+
+def blk_step(factors, grad, mom):
+    matrices, count, rows, columns = mom.shape
+    block = (1, 1, rows, columns)
+    whole = pl.BlockSpec(block, lambda m, c, f: (m, c, 0, 0))
+    shape = jax.ShapeDtypeStruct(mom.shape, jnp.bfloat16)
+    return pl.pallas_call(
+        blk_body,
+        out_shape=(shape, shape),
+        grid_spec=pltpu.PrefetchScalarGridSpec(
+            num_scalar_prefetch=1,
+            grid=(matrices, count),
+            in_specs=[pl.BlockSpec(block, lambda m, c, f: (c, m, 0, 0)), whole],
+            out_specs=[whole, whole],
+        ),
+        compiler_params=pltpu.CompilerParams(vmem_limit_bytes=vmem_bytes),
+        cost_estimate=pl.CostEstimate(
+            flops=8 * mom.size, bytes_accessed=8 * mom.size, transcendentals=mom.size
+        ),
+    )(factors, grad, mom)
 
 
 def on_device(emb_grad, emb_mom, blk_grad, blk_mom, tile_group, clip_rms):
@@ -39,11 +141,19 @@
     )
     owner_block = dp_index * row_blocks + mp_index * owner_rows // block_height
     owner_ids = lax.dynamic_index_in_dim(onehot, owner_block, axis=1, keepdims=False)
-    grad_pieces = blk_grad.reshape(matrices, mp_count, owner_rows, block_cols)
-    blk_owner = lax.all_to_all(grad_pieces, "mp", split_axis=1, concat_axis=1, tiled=True)
+
+    emb_to, emb_from = partner_tables(dp_count)
     emb_pieces = emb_grad.reshape(dp_count, own_rows, feature_block)
     mom_local = emb_mom.reshape(dp_count, own_rows, feature_block)
-    emb_owner = lax.all_to_all(emb_pieces, "dp", split_axis=0, concat_axis=0, tiled=True)
+    emb_got = []
+    for k in range(1, dp_count):
+        piece = lax.dynamic_index_in_dim(emb_pieces, emb_to(dp_index, k), axis=0, keepdims=False)
+        emb_got.append(lax.ppermute(piece, "dp", [(i, emb_to(i, k)) for i in range(dp_count)]))
+    blk_pieces = jnp.swapaxes(
+        blk_grad.reshape(matrices, mp_count, owner_rows, block_cols), 0, 1
+    )
+    blk_owner = lax.all_to_all(blk_pieces, "mp", split_axis=0, concat_axis=0, tiled=True)
+
     emb_squares = jnp.sum(jnp.square(emb_grad.astype(jnp.float32)))
     block_squares = jnp.sum(
         jnp.square(blk_grad.astype(jnp.float32)).reshape(
@@ -59,14 +169,16 @@
     root_mean = jnp.sqrt(totals / jnp.maximum(counts, 1.0))
     factor = jnp.minimum(1.0, clip_rms / (root_mean + epsilon))
     owner_factor = jnp.sum(owner_ids * factor, axis=-1)
-    clipped = blk_owner.astype(jnp.float32) * owner_factor[:, :, None, None]
-    blk_update, blk_moment = lion_step(clipped, blk_mom)
-    emb_update, emb_moment = lion_step(emb_owner.astype(jnp.float32) * factor[0], mom_local)
+
+    emb_sources = jnp.stack([emb_from(dp_index, k) for k in range(dp_count)]).astype(jnp.int32)
+    block = pl.cdiv(pl.cdiv(own_rows, 3), 16) * 16
+    blk_outs = blk_step(owner_factor, blk_owner, blk_mom)
+    emb_outs = emb_step(emb_sources, factor, emb_pieces, emb_got, mom_local, block)
     return (
-        emb_update.reshape(emb_mom.shape),
-        emb_moment.reshape(emb_mom.shape),
-        blk_update,
-        blk_moment,
+        emb_outs[0].reshape(emb_mom.shape),
+        emb_outs[1].reshape(emb_mom.shape),
+        blk_outs[0],
+        blk_outs[1],
     )
 
 

time: 469 us -> 312 us (0.67)
  waiting for transfers between devices: 164 us -> 0.01 us
  Pallas kernels: 0 us -> 50.6 us
  other arithmetic: 60.8 us -> 18.5 us
  blocking collectives: 190 us -> 199 us
  local copies, waits for them, and re-layouts: 35.6 us -> 30.1 us
  starting transfers between devices: 13.5 us -> 8.29 us
    all_to_all x2 -> x1, waiting for transfers between devices: 164 us -> 0.01 us  [on_device(): lax.all_to_all(blk_pieces, 'mp', split_axis=0, concat_axis=0, tiled=True)]
    pallas_call x0 -> x2, Pallas kernels: none -> 50.6 us  [the longest x1 31.3 us: emb_step(): pl.pallas_call(functools.partial(emb_body, count), out_shape=(shape, shap...]
    reshape x1 -> x0, other arithmetic: 28.6 us -> none  [on_device(): emb_moment.reshape(emb_mom.shape)]
    unnamed x8, local copies, waits for them, and re-layouts: 27.6 us -> 12.5 us
    convert_element_type x1 -> x0, other arithmetic: 15 us -> none  [lion_step(): (beta_second * moment + (1.0 - beta_second) * clipped).astype(jnp.bfloat16)]
    squeeze x0 -> x1, local copies, waits for them, and re-layouts: none -> 9.78 us  [on_device(): lax.dynamic_index_in_dim(emb_pieces, emb_to(dp_index, k), axis=0, keepdim...]
    psum x1, blocking collectives: 190 us -> 199 us  [on_device(): totals = lax.psum(partial_value, ('dp', 'mp'))]
    all_to_all x2 -> x1, starting transfers between devices: 13.5 us -> 5.64 us  [on_device(): lax.all_to_all(blk_pieces, 'mp', split_axis=0, concat_axis=0, tiled=True)]
  transfers between devices with their start and end apart: 2 -> 4, of which waited for: 1 -> 0; matrix products, arithmetic and copies ran while one was open for 14% -> 9% of each run, Pallas kernels for 0% -> 10%
where the time goes in v2:
time: 312 us; the launch traced here: 307 us
  blocking collectives  199 us (64%)
  Pallas kernels  50.6 us (16%)
  local copies, waits for them, and re-layouts  30.1 us (10%)
  other arithmetic  18.5 us (6%)
  starting transfers between devices  8.29 us (3%)
    psum x1, blocking collectives, on_device(): totals = lax.psum(partial_value, ('dp', 'mp'))  199 us
    pallas_call x1, Pallas kernels, emb_step(): pl.pallas_call(functools.partial(emb_body, count), out_shape=(shape, shap...  31.3 us
    pallas_call x1, Pallas kernels, blk_step(): pl.pallas_call(blk_body, out_shape=(shape, shape), grid_spec=pltpu.Prefet...  19.4 us
    unnamed x8, local copies, waits for them, and re-layouts  12.5 us
    reduce_sum x1, other arithmetic, on_device(): emb_squares = jnp.sum(jnp.square(emb_grad.astype(jnp.float32)))  11.1 us
    squeeze x1, local copies, waits for them, and re-layouts, on_device(): lax.dynamic_index_in_dim(emb_pieces, emb_to(dp_index, k), axis=0, keepdim...  9.78 us
    reshape x1, local copies, waits for them, and re-layouts, on_device(): blk_grad.reshape(matrices, mp_count, owner_rows, block_cols)  7.59 us
  transfers between devices with their start and end apart: 4, of which 0 were waited for; matrix products, arithmetic and copies ran while one was open for 9% of the time, Pallas kernels for 10%

profile of v2, /device:TPU:9, one launch (start us, length us, event | category | flops | bytes accessed | tf_op | source)
XLA Modules:
  0.0 307.0 jit_solution(13908605887627616024)
XLA Ops:
  0.6 12.5 %copy.22 = bf16[2,896,2368]{2,1,0:T(8,128)(2,1)} copy(bf16[2,896,2368]{1,2,0:T(8,128)(2,1)} %param.8) | data formatting | bytes 16973824 | tf_op args[2]
  13.1 7.6 %copy.27 = bf16[2,8,112,2368]{3,2,0,1:T(8,128)(2,1)} copy(bf16[2,8,112,2368]{3,2,1,0:T(8,128)(2,1)} %bitcast.33) | data formatting | bytes 16973824 | tf_op jit(solution)/shard_map/reshape | solution.py:153
  20.7 5.6 %all-to-all-start = ((bf16[8,2,112,2368]{3,2,1,0:T(8,128)(2,1)}), bf16[8,2,112,2368]{3,2,1,0:T(8,128)(2,1)}, u32[]{:S(2)}, u32[]{:S(2)}) async-start(bf16[8,2,112,2368]{3,2,1,0:T(8,128)(2,1)} %bitcast.32), calls=%async_computation | async-start | bytes 17432576 | tf_op jit(solution)/shard_map/all_to_all | solution.py:155
  26.3 0.0 copy-start
  26.3 9.8 %dynamic-slice_bitcast_fusion = (bf16[2376,896]{1,0:T(8,128)(2,1)}, bf16[2376,896]{1,0:T(8,128)(2,1)}, bf16[2376,896]{1,0:T(8,128)(2,1)}) fusion(bf16[4,2376,896]{2,1,0:T(8,128)(2,1)} %bitcast.30, s32[]{:T(128)S(6)} %select_n.36, s32[]{:T(128)S(6)} %select_n.35, s32[]{:T(128)S(6)} %select_n.34), kind=kLoop, calls=%fused_computation.3 | loop fusion | bytes 25546764 | tf_op jit(solution)/shard_map/jit(dynamic_index_in_dim)/squeeze | solution.py:150
  36.1 1.2 collective-permute-start
  37.3 1.2 collective-permute-start.1
  38.5 0.2 collective-permute-start.2
  38.7 0.0 copy-done
  38.8 0.1 constant_dynamic-slice_fusion
  38.8 0.1 copy.21
  39.0 5.1 %multiply_reduce_fusion.1 = f32[2,896]{1,0:T(2,128)S(1)} fusion(bf16[2,896,2368]{1,2,0:T(8,128)(2,1)} %param.8), kind=kLoop, calls=%fused_computation.1 | loop fusion | flops 12728576 | bytes 8494080 | tf_op jit(solution)/shard_map/reduce_sum | solution.py:158
  44.1 0.0 copy-start.2
  44.1 0.1 reduce_sum.53
  44.2 0.1 reduce_sum.54
  44.3 0.1 fusion.3
  44.4 11.1 %multiply_reduce_fusion = f32[]{:T(128)} fusion(bf16[9504,896]{1,0:T(8,128)(2,1)} %param.6), kind=kLoop, calls=%fused_computation | loop fusion | flops 25546752 | bytes 17031172 | tf_op jit(solution)/shard_map/reduce_sum | solution.py:157
  55.5 0.6 fusion.4
  56.1 198.8 %psum.7 = f32[4]{0:T(128)S(1)} all-reduce(f32[4]{0:T(128)S(1)} %fusion.4), channel_id=1, replica_groups=mesh['dp'=4,'mp'=8] {'dp','mp'}, use_global_device_ids=true, to_apply=%region_4.5 | all-reduce | flops 4 | bytes 32 | tf_op jit(solution)/shard_map/psum | solution.py:168
  254.9 0.6 pad_add_fusion.sources
  255.5 0.1 fusion.1
  255.7 0.0 copy-done.2
  255.7 0.0 copy-start.1
  255.7 0.7 fusion.2.factors
  256.4 0.0 collective-permute-done.refs_1_
  256.4 0.0 collective-permute-done.1.refs_2_
  256.4 0.0 collective-permute-done.2.refs_3_
  256.4 0.0 copy-done.1
  256.4 31.3 %shard_map.93 = (bf16[4,2376,896]{2,1,0:T(8,128)(2,1)}, bf16[4,2376,896]{2,1,0:T(8,128)(2,1)}) custom-call(s32[4]{0:T(128)} %pad_add_fusion.sources, f32[4]{0:T(128)} %copy-done.1, bf16[4,2376,896]{2,1,0:T(8,128)(2,1)} %bitcast.31, bf16[2376,896]{1,0:T(8,128)(2,1)} %collective-permute-done.refs_1_, bf16[2376,896]{1,0:T(8,128)(2,1)} %collective-permute-done.1.refs_2_, ...), custom_call_target="tpu_custom_call" | custom-call | flops 68124672 | bytes 68124672 | tf_op jit(solution)/shard_map/pallas_call | solution.py:81
  287.7 0.0 all-to-all-done.grad
  287.7 19.4 %shard_map.94 = (bf16[2,8,112,2368]{3,2,1,0:T(8,128)(2,1)}, bf16[2,8,112,2368]{3,2,1,0:T(8,128)(2,1)}) custom-call(f32[2,8]{1,0:T(2,128)} %fusion.2.factors, bf16[8,2,112,2368]{3,2,1,0:T(8,128)(2,1)} %all-to-all-done.grad, bf16[2,8,112,2368]{3,2,1,0:T(8,128)(2,1)} %moment.1), custom_call_target="tpu_custom_call" | custom-call | flops 33947648 | bytes 33947648 | tf_op jit(solution)/shard_map/pallas_call | solution.py:107
  (3 shorter events, 0.0 us)
Async XLA Ops:
  20.7 267.0 %all-to-all-start = ((bf16[8,2,112,2368]{3,2,1,0:T(8,128)(2,1)}), bf16[8,2,112,2368]{3,2,1,0:T(8,128)(2,1)}, u32[]{:S(2)}, u32[]{:S(2)}) async-start(bf16[8,2,112,2368]{3,2,1,0:T(8,128)(2,1)} %bitcast.32), calls=%async_computation | async-start | bytes 17432576 | tf_op jit(solution)/shard_map/all_to_all | solution.py:155
  26.3 12.4 %copy-start = (s32[2,8,8]{2,1,0:T(8,128)S(1)}, s32[2,8,8]{2,1,0:T(8,128)}, u32[]{:S(2)}) copy-start(s32[2,8,8]{2,1,0:T(8,128)} %param.10) | copy-start | bytes 1540
  36.1 220.3 %collective-permute-start = (bf16[2376,896]{1,0:T(8,128)(2,1)}, bf16[2376,896]{1,0:T(8,128)(2,1)}, u32[]{:S(2)}, u32[]{:S(2)}) collective-permute-start(bf16[2376,896]{1,0:T(8,128)(2,1)} %get-tuple-element.26), channel_id=1, source_target_pairs={{0,8},{8,0},{16,24},{24,16},{1,9},{9,1},{17,25},{25,17},{2,10},{10... | collective-permute-start | bytes 12773384 | tf_op jit(solution)/shard_map/ppermute | solution.py:151
  37.3 219.1 %collective-permute-start.1 = (bf16[2376,896]{1,0:T(8,128)(2,1)}, bf16[2376,896]{1,0:T(8,128)(2,1)}, u32[]{:S(2)}, u32[]{:S(2)}) collective-permute-start(bf16[2376,896]{1,0:T(8,128)(2,1)} %get-tuple-element.25), channel_id=1, source_target_pairs={{0,16},{8,24},{16,0},{24,8},{1,17},{9,25},{17,1},{25,9},{2,18},{10... | collective-permute-start | bytes 12773384 | tf_op jit(solution)/shard_map/ppermute | solution.py:151
  38.5 217.8 %collective-permute-start.2 = (bf16[2376,896]{1,0:T(8,128)(2,1)}, bf16[2376,896]{1,0:T(8,128)(2,1)}, u32[]{:S(2)}, u32[]{:S(2)}) collective-permute-start(bf16[2376,896]{1,0:T(8,128)(2,1)} %get-tuple-element.24), channel_id=1, source_target_pairs={{0,24},{8,16},{16,8},{24,0},{1,25},{9,17},{17,9},{25,1},{2,26},{10... | collective-permute-start | bytes 12773384 | tf_op jit(solution)/shard_map/ppermute | solution.py:151
  44.1 211.6 %copy-start.2 = (f32[4]{0:T(128)S(1)}, f32[4]{0:T(128)}, u32[]{:S(2)}) copy-start(f32[4]{0:T(128)} %param.11) | copy-start | bytes 52
  255.7 0.7 copy-start.1

commit v3 on v2

--- a/solution.py
+++ b/solution.py
@@ -146,11 +146,15 @@
     emb_pieces = emb_grad.reshape(dp_count, own_rows, feature_block)
     mom_local = emb_mom.reshape(dp_count, own_rows, feature_block)
     emb_got = []
-    for k in range(1, dp_count):
-        piece = lax.dynamic_index_in_dim(emb_pieces, emb_to(dp_index, k), axis=0, keepdims=False)
+    cut = [
+        lax.dynamic_index_in_dim(emb_pieces, emb_to(dp_index, k), axis=0, keepdims=False)
+        for k in range(1, dp_count)
+    ]
+    cut, blk_sent = lax.optimization_barrier((cut, blk_grad))
+    for k, piece in enumerate(cut, 1):
         emb_got.append(lax.ppermute(piece, "dp", [(i, emb_to(i, k)) for i in range(dp_count)]))
     blk_pieces = jnp.swapaxes(
-        blk_grad.reshape(matrices, mp_count, owner_rows, block_cols), 0, 1
+        blk_sent.reshape(matrices, mp_count, owner_rows, block_cols), 0, 1
     )
     blk_owner = lax.all_to_all(blk_pieces, "mp", split_axis=0, concat_axis=0, tiled=True)
 

time: 312 us -> 312 us (level)
    unnamed x8 -> x7, local copies, waits for them, and re-layouts: 12.5 us -> 0.02 us
    optimization_barrier x0 -> x1, local copies, waits for them, and re-layouts: none -> 12.4 us  [on_device(): cut, blk_sent = lax.optimization_barrier((cut, blk_grad))]
  transfers between devices with their start and end apart: 4 -> 4, of which waited for: 0 -> 0; matrix products, arithmetic and copies ran while one was open for 9% -> 6% of each run, Pallas kernels for 10% -> 10%
where the time goes in v3:
time: 312 us; the launch traced here: 307 us
  blocking collectives  199 us (64%)
  Pallas kernels  50.6 us (16%)
  local copies, waits for them, and re-layouts  30.1 us (10%)
  other arithmetic  18.4 us (6%)
  starting transfers between devices  8.42 us (3%)
    psum x1, blocking collectives, on_device(): totals = lax.psum(partial_value, ('dp', 'mp'))  199 us
    pallas_call x1, Pallas kernels, emb_step(): pl.pallas_call(functools.partial(emb_body, count), out_shape=(shape, shap...  31.3 us
    pallas_call x1, Pallas kernels, blk_step(): pl.pallas_call(blk_body, out_shape=(shape, shape), grid_spec=pltpu.Prefet...  19.4 us
    optimization_barrier x1, local copies, waits for them, and re-layouts, on_device(): cut, blk_sent = lax.optimization_barrier((cut, blk_grad))  12.4 us
    reduce_sum x1, other arithmetic, on_device(): emb_squares = jnp.sum(jnp.square(emb_grad.astype(jnp.float32)))  11.1 us
    squeeze x1, local copies, waits for them, and re-layouts, on_device(): lax.dynamic_index_in_dim(emb_pieces, emb_to(dp_index, k), axis=0, keepdim...  9.74 us
    reshape x1, local copies, waits for them, and re-layouts, on_device(): blk_sent.reshape(matrices, mp_count, owner_rows, block_cols)  7.59 us
  transfers between devices with their start and end apart: 4, of which 0 were waited for; matrix products, arithmetic and copies ran while one was open for 6% of the time, Pallas kernels for 10%

profile of v3, /device:TPU:9, one launch (start us, length us, event | category | flops | bytes accessed | tf_op | source)
XLA Modules:
  0.0 307.1 jit_solution(15953321383769397489)
XLA Ops:
  0.7 9.7 %dynamic-slice_bitcast_fusion = (bf16[2376,896]{1,0:T(8,128)(2,1)}, bf16[2376,896]{1,0:T(8,128)(2,1)}, bf16[2376,896]{1,0:T(8,128)(2,1)}) fusion(bf16[4,2376,896]{2,1,0:T(8,128)(2,1)} %bitcast.30, s32[]{:T(128)S(6)} %select_n.36, s32[]{:T(128)S(6)} %select_n.35, s32[]{:T(128)S(6)} %select_n.34), kind=kLoop, calls=%fused_computation.3 | loop fusion | bytes 25546764 | tf_op jit(solution)/shard_map/jit(dynamic_index_in_dim)/squeeze | solution.py:150
  10.4 12.4 %copy.22 = bf16[2,896,2368]{2,1,0:T(8,128)(2,1)} copy(bf16[2,896,2368]{1,2,0:T(8,128)(2,1)} %param.8) | data formatting | bytes 16973824 | tf_op jit(solution)/shard_map/optimization_barrier | solution.py:153
  22.8 7.6 %copy.27 = bf16[2,8,112,2368]{3,2,0,1:T(8,128)(2,1)} copy(bf16[2,8,112,2368]{3,2,1,0:T(8,128)(2,1)} %bitcast.33) | data formatting | bytes 16973824 | tf_op jit(solution)/shard_map/reshape | solution.py:157
  30.4 0.0 copy-start
  30.4 5.8 %all-to-all-start = ((bf16[8,2,112,2368]{3,2,1,0:T(8,128)(2,1)}), bf16[8,2,112,2368]{3,2,1,0:T(8,128)(2,1)}, u32[]{:S(2)}, u32[]{:S(2)}) async-start(bf16[8,2,112,2368]{3,2,1,0:T(8,128)(2,1)} %bitcast.32), calls=%async_computation | async-start | bytes 17432576 | tf_op jit(solution)/shard_map/all_to_all | solution.py:159
  36.2 1.2 collective-permute-start
  37.4 1.2 collective-permute-start.1
  38.7 0.2 collective-permute-start.2
  38.9 0.0 copy-done
  38.9 0.1 constant_dynamic-slice_fusion
  39.0 0.1 copy.21
  39.1 5.1 %multiply_reduce_fusion.1 = f32[2,896]{1,0:T(2,128)S(1)} fusion(bf16[2,896,2368]{1,2,0:T(8,128)(2,1)} %param.8), kind=kLoop, calls=%fused_computation.1 | loop fusion | flops 12728576 | bytes 8494080 | tf_op jit(solution)/shard_map/reduce_sum | solution.py:162
  44.2 0.0 copy-start.2
  44.2 0.1 reduce_sum.53
  44.3 0.1 reduce_sum.54
  44.4 0.1 fusion.3
  44.5 11.1 %multiply_reduce_fusion = f32[]{:T(128)} fusion(bf16[9504,896]{1,0:T(8,128)(2,1)} %param.6), kind=kLoop, calls=%fused_computation | loop fusion | flops 25546752 | bytes 17031172 | tf_op jit(solution)/shard_map/reduce_sum | solution.py:161
  55.6 0.6 fusion.4
  56.2 198.8 %psum.7 = f32[4]{0:T(128)S(1)} all-reduce(f32[4]{0:T(128)S(1)} %fusion.4), channel_id=1, replica_groups=mesh['dp'=4,'mp'=8] {'dp','mp'}, use_global_device_ids=true, to_apply=%region_4.5 | all-reduce | flops 4 | bytes 32 | tf_op jit(solution)/shard_map/psum | solution.py:172
  255.1 0.6 pad_add_fusion.sources
  255.6 0.1 fusion.1
  255.8 0.0 copy-done.2
  255.8 0.0 copy-start.1
  255.8 0.6 fusion.2.factors
  256.4 0.0 collective-permute-done.refs_1_
  256.4 0.0 collective-permute-done.1.refs_2_
  256.4 0.0 collective-permute-done.2.refs_3_
  256.4 0.0 copy-done.1
  256.5 31.3 %shard_map.93 = (bf16[4,2376,896]{2,1,0:T(8,128)(2,1)}, bf16[4,2376,896]{2,1,0:T(8,128)(2,1)}) custom-call(s32[4]{0:T(128)} %pad_add_fusion.sources, f32[4]{0:T(128)} %copy-done.1, bf16[4,2376,896]{2,1,0:T(8,128)(2,1)} %bitcast.31, bf16[2376,896]{1,0:T(8,128)(2,1)} %collective-permute-done.refs_1_, bf16[2376,896]{1,0:T(8,128)(2,1)} %collective-permute-done.1.refs_2_, ...), custom_call_target="tpu_custom_call" | custom-call | flops 68124672 | bytes 68124672 | tf_op jit(solution)/shard_map/pallas_call | solution.py:81
  287.7 0.0 all-to-all-done.grad
  287.7 19.4 %shard_map.94 = (bf16[2,8,112,2368]{3,2,1,0:T(8,128)(2,1)}, bf16[2,8,112,2368]{3,2,1,0:T(8,128)(2,1)}) custom-call(f32[2,8]{1,0:T(2,128)} %fusion.2.factors, bf16[8,2,112,2368]{3,2,1,0:T(8,128)(2,1)} %all-to-all-done.grad, bf16[2,8,112,2368]{3,2,1,0:T(8,128)(2,1)} %moment.1), custom_call_target="tpu_custom_call" | custom-call | flops 33947648 | bytes 33947648 | tf_op jit(solution)/shard_map/pallas_call | solution.py:107
  (3 shorter events, 0.0 us)
Async XLA Ops:
  30.4 8.4 %copy-start = (s32[2,8,8]{2,1,0:T(8,128)S(1)}, s32[2,8,8]{2,1,0:T(8,128)}, u32[]{:S(2)}) copy-start(s32[2,8,8]{2,1,0:T(8,128)} %param.10) | copy-start | bytes 1540
  30.4 257.3 %all-to-all-start = ((bf16[8,2,112,2368]{3,2,1,0:T(8,128)(2,1)}), bf16[8,2,112,2368]{3,2,1,0:T(8,128)(2,1)}, u32[]{:S(2)}, u32[]{:S(2)}) async-start(bf16[8,2,112,2368]{3,2,1,0:T(8,128)(2,1)} %bitcast.32), calls=%async_computation | async-start | bytes 17432576 | tf_op jit(solution)/shard_map/all_to_all | solution.py:159
  36.2 220.2 %collective-permute-start = (bf16[2376,896]{1,0:T(8,128)(2,1)}, bf16[2376,896]{1,0:T(8,128)(2,1)}, u32[]{:S(2)}, u32[]{:S(2)}) collective-permute-start(bf16[2376,896]{1,0:T(8,128)(2,1)} %get-tuple-element.12), channel_id=1, source_target_pairs={{0,8},{8,0},{16,24},{24,16},{1,9},{9,1},{17,25},{25,17},{2,10},{10... | collective-permute-start | bytes 12773384 | tf_op jit(solution)/shard_map/ppermute | solution.py:155
  37.4 219.0 %collective-permute-start.1 = (bf16[2376,896]{1,0:T(8,128)(2,1)}, bf16[2376,896]{1,0:T(8,128)(2,1)}, u32[]{:S(2)}, u32[]{:S(2)}) collective-permute-start(bf16[2376,896]{1,0:T(8,128)(2,1)} %get-tuple-element.13), channel_id=1, source_target_pairs={{0,16},{8,24},{16,0},{24,8},{1,17},{9,25},{17,1},{25,9},{2,18},{10... | collective-permute-start | bytes 12773384 | tf_op jit(solution)/shard_map/ppermute | solution.py:155
  38.7 217.8 %collective-permute-start.2 = (bf16[2376,896]{1,0:T(8,128)(2,1)}, bf16[2376,896]{1,0:T(8,128)(2,1)}, u32[]{:S(2)}, u32[]{:S(2)}) collective-permute-start(bf16[2376,896]{1,0:T(8,128)(2,1)} %get-tuple-element.14), channel_id=1, source_target_pairs={{0,24},{8,16},{16,8},{24,0},{1,25},{9,17},{17,9},{25,1},{2,26},{10... | collective-permute-start | bytes 12773384 | tf_op jit(solution)/shard_map/ppermute | solution.py:155
  44.2 211.6 %copy-start.2 = (f32[4]{0:T(128)S(1)}, f32[4]{0:T(128)}, u32[]{:S(2)}) copy-start(f32[4]{0:T(128)} %param.11) | copy-start | bytes 52
  255.8 0.6 copy-start.1
